TPU v7x, 512 devices: a whole 4x4x16 slice. The times are simulated.
512 devices in a mesh: blk: 32 (over y_lo, z), rows: 16 (over x, y_hi, core).
Axes of the slice: x: 4, y: 4 (y_hi: 2, y_lo: 2; y = y_hi * 2 + y_lo), z: 16, core: 2. Of those that a mesh axis runs over, the one named last changes fastest.
Arguments:
- snapshots: bfloat16 [4096, 8192], P('blk', 'rows'), may hold values from -6 to 6
- node_owner: int32 [8192, 1], P('rows'), may hold values from 0 to 15; in each aligned block of 512 rows (0 to 511, 512 to 1023, ...) at most 128 rows name the same one
- mass_blocks: bfloat16 [16, 64, 128, 128], P('rows', 'blk'), as said below
- mass_cols: int32 [16, 64], P('rows', 'blk'), may hold values from 0 to 15, as said below
Outputs:
- gram: float32 [4096, 4096], P('rows', 'blk')
Inputs may be any that keep to these rules, and one draw needn't show every extreme that they name: `node_owner`: of the nodes of one evolution partition, at most 128 go to one owner, and exactly 128 do for some owner. `mass_cols`: the stored blocks of row block r of an owner have the column blocks r, r - 1 or r, r + 1 or r, and r, in this order; a block whose column is r in any slot but the first is zero. `mass_blocks`: each owner's M_d is symmetric with a positive diagonal that dominates every row.
All inputs are finite; a program needn't handle non-finite values.
Results may differ from a plain program's by a relative error of at most 0.0005.
Values may be sent and summed in bfloat16 or wider, within the bound.
A program may use at most 64 MiB of HBM per device.

v0:
```python
import jax
import jax.numpy as jnp
from jax import lax
from jax.sharding import PartitionSpec as P

KB = 4


def per_device(snapshots, node_owner, mass_blocks, mass_cols):
    owners = lax.axis_size("rows")
    snap_dev = snapshots.shape[0]
    node_dev = snapshots.shape[1]
    capacity = 4 * node_dev // owners
    slot_count = owners * capacity
    block_size = mass_blocks.shape[-1]
    row_blocks = slot_count // block_size
    dest = node_owner[:, 0]
    owner_ids = jnp.arange(owners, dtype=jnp.int32)
    onehot = (dest[:, None] == owner_ids[None, :]).astype(jnp.int32)
    before = jnp.cumsum(onehot, axis=0) - onehot
    rank = jnp.sum(before * onehot, axis=1)
    target = dest * capacity + rank
    source_of = (
        jnp.zeros((slot_count,), jnp.int32).at[target].set(jnp.arange(node_dev, dtype=jnp.int32))
    )
    filled = jnp.zeros((slot_count,), jnp.bool_).at[target].set(True)
    outgoing = jnp.where(
        filled[None, :], jnp.take(snapshots, source_of, axis=1), jnp.zeros((), jnp.bfloat16)
    )
    slab = lax.all_to_all(outgoing, "rows", split_axis=1, concat_axis=1, tiled=True)
    split_rows = slab.reshape(snap_dev, row_blocks, block_size)
    block_ids = jnp.arange(row_blocks, dtype=jnp.int32)
    col_wire = mass_cols[0].astype(jnp.bfloat16)
    blocks = lax.all_gather(mass_blocks[0], "blk", axis=0, tiled=True)
    col_values = lax.all_gather(col_wire, "blk", axis=0, tiled=True)
    count = blocks.shape[0]
    which_row = jnp.arange(count, dtype=jnp.int32) // KB
    picked = jnp.take(split_rows, which_row, axis=1)
    product = jnp.einsum("smi,mij->smj", picked, blocks, preferred_element_type=jnp.float32)
    cols = col_values.astype(jnp.int32)
    placed = (cols[:, None] == block_ids[None, :]).astype(jnp.float32)
    mapped = jnp.einsum("smj,mn->snj", product, placed)
    weighted = mapped.reshape(snap_dev, slot_count).astype(jnp.bfloat16)
    contract = (((1,), (1,)), ((), ()))
    tile = lax.dot_general(
        lax.all_gather(weighted, "blk", axis=0, tiled=True),
        slab,
        contract,
        preferred_element_type=jnp.float32,
    )
    gram = lax.psum_scatter(tile, "rows", scatter_dimension=0, tiled=True)
    return gram


def solution(mesh):
    placed = (P("blk", "rows"), P("rows", None), P("rows", "blk", None, None), P("rows", "blk"))
    return jax.shard_map(
        per_device, mesh=mesh, in_specs=placed, out_specs=P("rows", "blk"), check_vma=False
    )
```

profile of v0, /device:TPU:6, one launch (start us, length us, event | category | flops | bytes accessed | tf_op | source)
XLA Modules:
  0.0 450.1 jit_solution(8701757486053184302)
XLA Ops:
  6.5 0.0 all-gather.7.cloned.1.call-start
  6.5 0.7 all-gather.7.cloned.1.call-update
  7.3 0.7 fusion.13
  7.9 1.1 reduce-window.6
  9.1 0.2 slice_reduce_fusion
  9.3 1.0 copy.18
  10.4 0.8 fusion.12
  11.2 0.7 compare_select_fusion.1
  11.8 2.4 scatter_custom_fusion.1
  14.3 6.2 %gather_fusion = bf16[2048,128]{1,0:T(8,128)(2,1)S(1)} fusion(bf16[128,512]{0,1:T(8,128)(2,1)S(1)} %copy.18, s32[2048]{0:T(1024)S(1)} %fusion.16), kind=kCustom, calls=%fused_computation | custom fusion | bytes 1056768 | tf_op jit(solution)/shard_map/jit(_take)/gather | solution.py:28
  20.5 0.0 copy-start
  20.5 0.3 copy.19
  20.8 2.4 scatter_custom_fusion
  23.3 0.9 select_select_fusion
  24.2 9.3 %all-to-all-start = ((bf16[128,16,128]{2,0,1:T(8,128)(2,1)}), bf16[128,16,128]{2,0,1:T(8,128)(2,1)S(1)}, u32[]{:S(2)}, u32[]{:S(2)}) async-start(bf16[128,16,128]{2,0,1:T(8,128)(2,1)} %select_select_fusion), calls=%async_computation | async-start | bytes 1048576 | tf_op jit(solution)/shard_map/all_to_all | solution.py:30
  33.4 0.0 all-gather.5.cloned.1.call-start
  33.5 1.3 dynamic-slice
  35.4 0.2 dynamic-update-slice
  35.7 67.8 %all-reduce = bf16[64]{0:T(256)(128)(2,1)S(1)} all-reduce(bf16[64]{0:T(256)(128)(2,1)S(1)} %dynamic-update-slice), channel_id=2, replica_groups=mesh['blk'=32,'rows'=16] {'blk'}, use_global_device_ids=true, to_apply=%add | all-reduce | flops 64 | bytes 256
  103.5 0.0 all-to-all-done
  103.5 1.0 gather_fusion.1
  104.5 43.0 %all-gather.7.cloned.1.call-done = bf16[1,64,128,128]{3,2,0,1:T(8,128)(2,1)} async-done(((bf16[1,2,128,128]{3,2,0,1:T(8,128)(2,1)}), bf16[1,64,128,128]{3,2,0,1:T(8,128)(2,1)}) %all-gather.7.cloned.1.call-update) | async-done | bytes 2097168 | tf_op jit(solution)/shard_map/all_gather | solution.py:34
  147.5 2.4 convolution_bitcast_fusion
  149.9 1.3 fusion.6
  151.1 0.9 copy.31
  152.0 0.0 all-gather.5.cloned.1.call-update
  152.1 0.0 reduce-scatter.2.cloned.1.call-start
  152.1 0.3 copy.22
  152.4 190.9 %all-gather.5.cloned.1.call-done = bf16[4096,2048]{1,0:T(8,128)(2,1)} async-done(((bf16[128,2048]{1,0:T(8,128)(2,1)}), bf16[4096,2048]{1,0:T(8,128)(2,1)}) %all-gather.5.cloned.1.call-update) | async-done | bytes 16777232 | tf_op jit(solution)/shard_map/all_gather | solution.py:46
  343.3 9.5 %fusion.24 = f32[4096,128]{1,0:T(8,128)} fusion(bf16[4096,2048]{1,0:T(8,128)(2,1)} %all-gather.5.cloned.1.call-done, bf16[128,2048]{0,1:T(8,128)(2,1)S(1)} %bitcast.59), kind=kOutput, calls=%fused_computation.50 | convolution fusion | flops 2147483648 | bytes 19398656 | tf_op jit(solution)/shard_map/dot_general | solution.py:45
  352.7 0.0 reduce-scatter.2.cloned.1.call-update
  352.8 90.8 %reduce-scatter.2.cloned.1.call-done = f32[256,128]{1,0:T(8,128)} async-done(((f32[4096,128]{1,0:T(8,128)}), f32[256,128]{1,0:T(8,128)}) %reduce-scatter.2.cloned.1.call-update) | async-done | bytes 131088 | tf_op jit(solution)/shard_map/reduce_scatter | solution.py:51
  (13 shorter events, 0.1 us)
Async XLA Ops:
  6.5 140.9 %all-gather.7.cloned.1.call-start = ((), (), s32[]{:S(2)}) async-start(), calls=%async_computation.4 | async-start | bytes 2162688 | tf_op jit(solution)/shard_map/all_gather | solution.py:34
  20.5 14.9 %copy-start = (s32[1,2]{1,0:T(1,128)S(1)}, s32[1,2]{1,0:T(1,128)}, u32[]{:S(2)}) copy-start(s32[1,2]{1,0:T(1,128)} %param.7) | copy-start | bytes 28
  24.2 79.4 %all-to-all-start = ((bf16[128,16,128]{2,0,1:T(8,128)(2,1)}), bf16[128,16,128]{2,0,1:T(8,128)(2,1)S(1)}, u32[]{:S(2)}, u32[]{:S(2)}) async-start(bf16[128,16,128]{2,0,1:T(8,128)(2,1)} %select_select_fusion), calls=%async_computation | async-start | bytes 1048576 | tf_op jit(solution)/shard_map/all_to_all | solution.py:30
  33.4 309.8 %all-gather.5.cloned.1.call-start = ((), (), s32[]{:S(2)}) async-start(), calls=%async_computation.2 | async-start | bytes 17301504 | tf_op jit(solution)/shard_map/all_gather | solution.py:46
  152.1 291.5 %reduce-scatter.2.cloned.1.call-start = ((), (), s32[]{:S(2)}) async-start(), calls=%async_computation.3 | async-start | bytes 2228224 | tf_op jit(solution)/shard_map/reduce_scatter | solution.py:51
Sparse Core Ops, SparseCore 0:
  9.4 137.9 all-gather.6
  152.2 191.0 all-gather.4
  352.9 90.6 reduce-scatter.1
where the time goes:
time: 451 us; the launch traced here: 450 us
  waiting for transfers between devices  325 us (72%)
  blocking collectives  67.8 us (15%)
  local copies, waits for them, and re-layouts  16.3 us (4%)
  between operations  13.9 us (3%)
  matrix products  13.1 us (3%)
  starting transfers between devices  9.37 us (2%)
    all_gather x1, waiting for transfers between devices, per_device(): lax.all_gather(weighted, 'blk', axis=0, tiled=True)  191 us
    reduce_scatter x1, waiting for transfers between devices, per_device(): gram = lax.psum_scatter(tile, 'rows', scatter_dimension=0, tiled=True)  90.8 us
    unnamed x1, blocking collectives  67.8 us
    all_gather x1, waiting for transfers between devices, per_device(): blocks = lax.all_gather(mass_blocks[0], 'blk', axis=0, tiled=True)  43 us
    dot_general x1, matrix products, per_device(): lax.dot_general(lax.all_gather(weighted, 'blk', axis=0, tiled=True), slab...  9.47 us
    all_to_all x1, starting transfers between devices, per_device(): lax.all_to_all(outgoing, 'rows', split_axis=1, concat_axis=1, tiled=True)  9.28 us
  transfers between devices with their start and end apart: 4, of which 3 were waited for; matrix products, arithmetic and copies ran while one was open for 4% of the time, Pallas kernels for 0%

commit v1 on v0

v1 whole, which is shorter than its diff:
```python
import jax
import jax.numpy as jnp
from jax import lax
from jax.experimental import pallas as pl
from jax.experimental.pallas import tpu as pltpu
from jax.sharding import PartitionSpec as P

MESH = pl.DeviceIdType.MESH
F32 = jnp.float32
BF16 = jnp.bfloat16
NZ = 16
NR = 16
ND = 512
SD = 128
T0 = (((0,), (0,)), ((), ()))
T1 = (((1,), (1,)), ((), ()))


def codes_of(raw, q):
    v = raw[q, 16:32, :].astype(F32)
    own = jnp.concatenate([v[i : i + 1, :] for i in range(4)], axis=1)
    rank = jnp.concatenate([v[i : i + 1, :] for i in range(4, 8)], axis=1)
    return own, rank


def onehot(row, n):
    ids = lax.broadcasted_iota(jnp.int32, (n, row.shape[1]), 0).astype(F32)
    return jnp.where(ids == row, 1.0, 0.0).astype(BF16)


def kernel(
    snap, owner, mass, out,
    msg, raw, mz, cbuf, halo, sall, acc, wown, wc, gt, yrecv, xsend, xrecv,
    t_send, t_recv, a_send, a_recv, b_send, b_recv, c_send, c_recv,
    h_send, h_recv, r_send, r_recv, l_send, l_recv, s_send, s_recv,
    w_send, w_recv, y_send, y_recv, x_send, x_recv,
):
    blk, s = lax.axis_index("blk"), lax.axis_index("rows")
    yl, z = blk // NZ, lax.rem(blk, NZ)
    x, yh, c = s // 4, lax.rem(s // 2, 2), lax.rem(s, 2)
    sib = s + 1 - 2 * c

    def zmove(k):
        return lax.rem(z + k + NZ, NZ)

    def to(src, dst, ssem, rsem, b, r):
        return pltpu.make_async_remote_copy(
            src_ref=src, dst_ref=dst, send_sem=ssem, recv_sem=rsem, device_id=(b, r), device_id_type=MESH
        )

    def drain(ref, sem):
        pltpu.make_async_copy(ref, ref, sem).wait()

    barrier = pltpu.get_barrier_semaphore()
    plane = yl * NR + s

    def greet(i, carry):
        other = lax.rem(plane + i, 2 * NR)
        pl.semaphore_signal(
            barrier, inc=1, device_id=((other // NR) * NZ + z, lax.rem(other, NR)), device_id_type=MESH
        )
        return carry

    lax.fori_loop(1, 2 * NR, greet, 0)
    for k in (1, -1, 2, -2, 4, -4, 8):
        pl.semaphore_signal(barrier, inc=1, device_id=(yl * NZ + zmove(k), s), device_id_type=MESH)

    own = owner[...].astype(F32)
    mine = onehot(own, NR)
    before = jnp.where(
        lax.broadcasted_iota(jnp.int32, (ND, ND), 0) < lax.broadcasted_iota(jnp.int32, (ND, ND), 1), 1.0, 0.0
    ).astype(BF16)
    counts = jnp.dot(mine, before, preferred_element_type=F32)
    rank = jnp.sum(mine.astype(F32) * counts, axis=0, keepdims=True)
    row = lax.broadcasted_iota(jnp.int32, (16, 128), 0)
    code = jnp.zeros((16, 128), F32)
    for i in range(4):
        code = jnp.where(row == i, own[:, 128 * i : 128 * i + 128], code)
        code = jnp.where(row == i + 4, rank[:, 128 * i : 128 * i + 128], code)
    code = code.astype(BF16)
    for a in range(NR):
        msg[a, 0:16, :] = mass[a]
        msg[a, 16:32, :] = code
    sall[c, z] = snap[...]
    halo[2 + yl] = snap[...]
    raw[s] = msg[s]

    pl.semaphore_wait(barrier, 2 * NR - 1 + 7)

    def scatter(i, carry):
        a = lax.rem(s + i, NR)
        to(msg.at[a], raw.at[s], t_send, t_recv, blk, a).start()
        return carry

    lax.fori_loop(1, NR, scatter, 0)

    def ring(k, h, right):
        slot = zmove(-(k - 1)) if right else zmove(k - 1)
        ref = sall.at[c, slot, pl.ds(64 * h, 64)]
        ss, rs = (r_send, r_recv) if right else (l_send, l_recv)
        return to(ref, ref, ss.at[k - 1, h], rs.at[k - 1, h], yl * NZ + zmove(1 if right else -1), s)

    def arrived(k, h, right):
        slot = zmove(-k) if right else zmove(k)
        ref = sall.at[c, slot, pl.ds(64 * h, 64)]
        rs = r_recv if right else l_recv
        pltpu.make_async_copy(ref, ref, rs.at[k - 1, h]).wait()

    def sibling(slot):
        ref = sall.at[c, slot]
        return to(ref, ref, s_send.at[slot], s_recv.at[slot], blk, sib)

    for h in range(2):
        for right in (True, False):
            ring(1, h, right).start()
    sibling(z).start()

    def halo_copy(dyl, ds):
        return to(
            snap, halo.at[2 - 2 * ds + yl], h_send.at[dyl, ds + 1], h_recv, lax.rem(yl + dyl, 2) * NZ + z, s + ds
        )

    def halo_each(f):
        for ds in (0, -1, 1):
            for dyl in (0, 1):
                if ds == 0 and dyl == 0:
                    continue
                if ds == 0:
                    f(halo_copy(dyl, ds))
                else:
                    pl.when(jnp.logical_and(s + ds >= 0, s + ds < NR))(lambda dyl=dyl, ds=ds: f(halo_copy(dyl, ds)))

    halo_each(lambda copy: copy.start())

    def ring_step(k):
        for h in range(2):
            for right in (True, False):
                if k == 8 and right != (h == 0):
                    continue
                arrived(k, h, right)
                if k < 7 or (k == 7 and right == (h == 0)):
                    ring(k + 1, h, right).start()
        sibling(zmove(-k)).start()
        if k < 8:
            sibling(zmove(k)).start()

    zt = lax.rem(z + 1, NZ)
    r_blk = yl * 8 + z // 2
    odd = lax.rem(z, 2)
    col = jnp.where(odd == 1, r_blk + 1, jnp.where(s >= 8, r_blk - 1, r_blk))
    col = jnp.clip(col, 0, NR - 1)
    drain(raw.at[0:15], t_recv)
    own_c, rank_c = codes_of(raw, col)
    slices = raw[:, 0:16, :].reshape(256, 128)
    picked = jnp.dot(slices, onehot(rank_c, 128), preferred_element_type=F32)
    kept = jnp.zeros((16, ND), F32)
    for d in range(NR):
        kept = jnp.where(own_c == float(d), picked[16 * d : 16 * d + 16, :], kept)
    mz[zt // 4, lax.rem(zt, 4)] = kept.astype(BF16)
    mine_z = mz.at[zt // 4, lax.rem(zt, 4)]
    for k in (4, -4, 8):
        to(mine_z, mine_z, a_send, a_recv, yl * NZ + zmove(k), s).start()
    ring_step(1)
    drain(mz.at[0:3, 0], a_recv)
    four = mz.at[:, lax.rem(zt, 4)]
    for k in (1, -1, 2):
        to(four, four, b_send, b_recv, yl * NZ + zmove(k), s).start()
    ring_step(2)
    drain(mz.at[:, 0:3], b_recv)

    def spread(f_remote, f_local):
        def send(src, kinds, slot, cc, dyl, sem):
            dst = cbuf.at[kinds, slot]
            here = jnp.logical_and(cc == s, dyl == 0)
            pl.when(jnp.logical_not(here))(
                lambda: f_remote(to(src, dst, sem, c_recv, lax.rem(yl + dyl, 2) * NZ + z, cc))
            )
            if f_local is not None:
                pl.when(here)(lambda: f_local(pltpu.make_async_copy(src, dst, c_recv)))

        def low(w, carry):
            for dyl in range(2):
                send(
                    mz.at[w // 2, pl.ds(2 * lax.rem(w, 2), 2)], pl.ds(0, 2), s, yl * 8 + w, dyl, c_send.at[w, dyl]
                )
            return carry

        def high(w, carry):
            cc = yl * 8 + w - 1

            @pl.when(cc >= 0)
            def _():
                for dyl in range(2):
                    send(mz.at[w // 2, 2 * lax.rem(w, 2) + 1], 2, s - 8, cc, dyl, c_send.at[w, dyl])

            return carry

        @pl.when(s < 8)
        def _():
            lax.fori_loop(1, 8, low, 0)
            for dyl in range(2):
                send(mz.at[0, 1], 1, s, yl * 8, dyl, c_send.at[0, dyl])

            @pl.when(yl == 0)
            def _():
                for dyl in range(2):
                    send(mz.at[0, 0], 0, s, 8 + 0 * yl, dyl, c_send.at[8, dyl])

        @pl.when(s >= 8)
        def _():
            lax.fori_loop(0, 8, high, 0)

    spread(lambda copy: copy.start(), lambda copy: copy.start())
    ring_step(3)

    edge = jnp.logical_or(s == 0, s == NR - 1)

    @pl.when(edge)
    def _():
        drain(halo.at[0:3], h_recv)
        drain(cbuf.at[0:2], c_recv)

    @pl.when(jnp.logical_not(edge))
    def _():
        drain(halo.at[0:5], h_recv)
        drain(cbuf, c_recv)

    acc[...] = jnp.zeros_like(acc)
    own_s, _ = codes_of(raw, s)
    hot_s = onehot(own_s, NR)

    def weigh(j):
        @pl.when(jnp.logical_and(s - 1 + j >= 0, s - 1 + j < NR))
        def _():
            own_j, rank_j = codes_of(raw, s - 1 + j)
            same = lax.dot_general(onehot(own_j, NR), hot_s, T0, preferred_element_type=F32)
            wide = lax.dot_general(onehot(rank_j, 128), cbuf[j].reshape(128, ND), T0, preferred_element_type=F32)
            m = (wide * same).astype(BF16)
            acc[...] += jnp.dot(halo[2 * j : 2 * j + 2].reshape(2 * SD, ND), m, preferred_element_type=F32)

    weigh(0)
    ring_step(4)
    weigh(1)
    ring_step(5)
    weigh(2)
    wown[...] = acc[...].reshape(2, SD, ND).astype(BF16)
    wc[c] = wown[c]
    w_copy = to(wown.at[1 - c], wc.at[c], w_send, w_recv, blk, sib)
    w_copy.start()
    ring_step(6)
    drain(wc.at[0], w_recv)

    def piece(zz, f):
        home = x * 4 + lax.rem(zz // 4, 2) * 2 + lax.rem(zz // 2, 2)
        dst = yrecv.at[yl, yh, zz // 8, lax.rem(zz, 2)]
        far = jnp.logical_or(home != s, c != yl)
        pl.when(far)(lambda: f(to(gt.at[zz], dst, y_send.at[zz], y_recv, c * NZ + z, home)))
        return jnp.logical_not(far), dst

    def tile(zz):
        drain(sall.at[1 - c, zz], s_recv.at[zz])
        g = lax.dot_general(sall[0, zz], wc[0], T1, preferred_element_type=F32)
        gt[zz] = g + lax.dot_general(sall[1, zz], wc[1], T1, preferred_element_type=F32)
        near, dst = piece(zz, lambda copy: copy.start())
        pl.when(near)(lambda: pltpu.make_async_copy(gt.at[zz], dst, y_recv).start())

    tile(z)
    for k in range(1, 7):
        tile(zmove(-k))
        tile(zmove(k))
    ring_step(7)
    tile(zmove(-7))
    tile(zmove(7))
    ring_step(8)
    tile(zmove(8))

    drain(yrecv, y_recv)
    for i in range(4):
        xsend[i] = (yrecv[i // 2, 0, i % 2] + yrecv[i // 2, 1, i % 2]).reshape(256, 128)
        pl.when(x != i)(
            lambda i=i: to(xsend.at[i], xrecv.at[x], x_send.at[i], x_recv, blk, 4 * i + 2 * yh + c).start()
        )
    xrecv[x] = xsend[x]
    drain(xrecv.at[0:3], x_recv)
    out[...] = (xrecv[0] + xrecv[1]) + (xrecv[2] + xrecv[3])

    drain(msg.at[0:15], t_send)
    drain(mz.at[0:3, 0], a_send)
    drain(mz.at[:, 0:3], b_send)
    spread(lambda copy: copy.wait_send(), None)
    halo_each(lambda copy: copy.wait_send())
    for k in range(1, 9):
        for h in range(2):
            for right in (True, False):
                if k < 8 or right == (h == 0):
                    ring(k, h, right).wait_send()

    def left(i, carry):
        sibling(i).wait_send()
        piece(i, lambda copy: copy.wait_send())
        return carry

    lax.fori_loop(0, NZ, left, 0)
    w_copy.wait_send()
    for i in range(4):
        pl.when(x != i)(
            lambda i=i: to(xsend.at[i], xrecv.at[x], x_send.at[i], x_recv, blk, 4 * i + 2 * yh + c).wait_send()
        )


def per_device(snapshots, node_owner, mass_blocks, mass_cols):
    dma = pltpu.SemaphoreType.DMA
    one = dma(())
    vmem = pl.BlockSpec(memory_space=pltpu.VMEM)
    return pl.pallas_call(
        kernel,
        out_shape=jax.ShapeDtypeStruct((256, 128), F32),
        in_specs=[vmem] * 3,
        out_specs=vmem,
        scratch_shapes=[
            pltpu.VMEM((16, 32, 128), BF16),
            pltpu.VMEM((16, 32, 128), BF16),
            pltpu.VMEM((4, 4, 16, ND), BF16),
            pltpu.VMEM((3, 8, 16, ND), BF16),
            pltpu.VMEM((6, SD, ND), BF16),
            pltpu.VMEM((2, NZ, SD, ND), BF16),
            pltpu.VMEM((2 * SD, ND), F32),
            pltpu.VMEM((2, SD, ND), BF16),
            pltpu.VMEM((2, SD, ND), BF16),
            pltpu.VMEM((NZ, 128, 128), F32),
            pltpu.VMEM((2, 2, 2, 2, 128, 128), F32),
            pltpu.VMEM((4, 256, 128), F32),
            pltpu.VMEM((4, 256, 128), F32),
            one, one, one, one, one, one, dma((9, 2)), one,
            dma((2, 3)), one, dma((8, 2)), dma((8, 2)), dma((8, 2)), dma((8, 2)), dma((NZ,)), dma((NZ,)),
            one, one, dma((NZ,)), one, dma((4,)), one,
        ],
        compiler_params=pltpu.CompilerParams(
            collective_id=0, has_side_effects=True, vmem_limit_bytes=48 * 1024 * 1024
        ),
        cost_estimate=pl.CostEstimate(flops=1200000000, bytes_accessed=400000, transcendentals=0),
    )(snapshots, node_owner.reshape(1, ND), mass_blocks.reshape(16, 16, 128))


def solution(mesh):
    placed = (P("blk", "rows"), P("rows", None), P("rows", "blk", None, None), P("rows", "blk"))
    return jax.shard_map(
        per_device, mesh=mesh, in_specs=placed, out_specs=P("rows", "blk"), check_vma=False
    )
```

time: 451 us -> 83 us (0.18)
  the two profiles are of different devices: /device:TPU:6 before, /device:TPU:69 now
where the time goes in v1:
time: 83 us; the launch traced here: 82.8 us
  Pallas kernels  79.7 us (96%)
  local copies, waits for them, and re-layouts  3.08 us (4%)
    pallas_call x1, Pallas kernels, per_device(): pl.pallas_call(kernel, out_shape=jax.ShapeDtypeStruct((256, 128), F32), i...  79.7 us
    unnamed x7, local copies, waits for them, and re-layouts  3.08 us

profile of v1, /device:TPU:69, one launch (start us, length us, event | category | flops | bytes accessed | tf_op | source)
XLA Modules:
  0.0 82.8 jit_solution(16486790692615459825)
XLA Ops:
  0.0 0.0 copy-start.2
  0.0 0.7 copy-done.2
  0.7 0.0 copy-start
  0.7 0.9 %copy-done = bf16[128,512]{1,0:T(8,128)(2,1)S(1)} copy-done((bf16[128,512]{1,0:T(8,128)(2,1)S(1)}, bf16[128,512]{1,0:T(8,128)(2,1)}, u32[]{:S(2)}) %copy-start) | copy-done | bytes 131096
  1.6 0.0 copy-start.1
  1.6 0.8 %copy-done.1 = bf16[1,2,128,128]{3,2,1,0:T(8,128)(2,1)S(1)} copy-done((bf16[1,2,128,128]{3,2,1,0:T(8,128)(2,1)S(1)}, bf16[1,2,128,128]{3,2,1,0:T(8,128)(2,1)}, u32[]{:S(2)}) %copy-start.1) | copy-done | bytes 65560
  2.4 79.7 %shard_map.37 = f32[256,128]{1,0:T(8,128)S(1)} custom-call(bf16[128,512]{1,0:T(8,128)(2,1)S(1)} %copy-done, s32[1,512]{1,0:T(1,128)S(1)} %bitcast.3, bf16[16,16,128]{2,1,0:T(8,128)(2,1)S(1)} %bitcast.2), custom_call_target="tpu_custom_call" | custom-call | flops 1200000000 | bytes 400000 | tf_op jit(solution)/shard_map/pallas_call | solution.py:315
  82.1 0.7 copy.5
Async XLA Ops:
  0.0 0.7 copy-start.2
  0.7 0.9 %copy-start = (bf16[128,512]{1,0:T(8,128)(2,1)S(1)}, bf16[128,512]{1,0:T(8,128)(2,1)}, u32[]{:S(2)}) copy-start(bf16[128,512]{1,0:T(8,128)(2,1)} %snap.1) | copy-start | bytes 393220
  1.6 0.8 %copy-start.1 = (bf16[1,2,128,128]{3,2,1,0:T(8,128)(2,1)S(1)}, bf16[1,2,128,128]{3,2,1,0:T(8,128)(2,1)}, u32[]{:S(2)}) copy-start(bf16[1,2,128,128]{3,2,1,0:T(8,128)(2,1)} %param.6) | copy-start | bytes 196612

commit v2 on v1

v2 whole, which is shorter than its diff:
```python
import jax
import jax.numpy as jnp
from jax import lax
from jax.experimental import pallas as pl
from jax.experimental.pallas import tpu as pltpu
from jax.sharding import PartitionSpec as P

MESH = pl.DeviceIdType.MESH
F32 = jnp.float32
BF16 = jnp.bfloat16
NZ = 16
NR = 16
ND = 512
SD = 128
NCH = 4
CH = SD // NCH
T0 = (((0,), (0,)), ((), ()))
T1 = (((1,), (1,)), ((), ()))


def codes_of(raw, q):
    v = raw[q, 16:32, :].astype(F32)
    own = jnp.concatenate([v[i : i + 1, :] for i in range(4)], axis=1)
    rank = jnp.concatenate([v[i : i + 1, :] for i in range(4, 8)], axis=1)
    return own, rank


def onehot(row, n):
    ids = lax.broadcasted_iota(jnp.int32, (n, row.shape[1]), 0).astype(F32)
    return jnp.where(ids == row, 1.0, 0.0).astype(BF16)


def kernel(
    snap, owner, mass, out,
    own_v, mass_v, msg, raw, mz, cbuf, halo, sall, acc, wown, wc, gt, yrecv, xsend, xrecv,
    i_sem, t_send, t_recv, a_send, a_recv, b_send, b_recv, c_send, c_recv,
    h_send, h_recv, z_send, r_recv, l_recv, s_send, s_recv,
    w_send, w_recv, y_send, y_recv, x_send, x_recv,
):
    blk, s = lax.axis_index("blk"), lax.axis_index("rows")
    yl, z = blk // NZ, lax.rem(blk, NZ)
    x, yh, c = s // 4, lax.rem(s // 2, 2), lax.rem(s, 2)
    sib = s + 1 - 2 * c

    def zmove(k):
        return lax.rem(z + k + NZ, NZ)

    def to(src, dst, ssem, rsem, b, r):
        return pltpu.make_async_remote_copy(
            src_ref=src, dst_ref=dst, send_sem=ssem, recv_sem=rsem, device_id=(b, r), device_id_type=MESH
        )

    def drain(ref, sem):
        pltpu.make_async_copy(ref, ref, sem).wait()

    barrier = pltpu.get_barrier_semaphore()
    for k in (8, 4, -4, 2, -2, 1, -1):
        pl.semaphore_signal(barrier, inc=1, device_id=(yl * NZ + zmove(k), s), device_id_type=MESH)
    plane = yl * NR + s

    def greet(i, carry):
        other = lax.rem(plane + i, 2 * NR)
        pl.semaphore_signal(
            barrier, inc=1, device_id=((other // NR) * NZ + z, lax.rem(other, NR)), device_id_type=MESH
        )
        return carry

    lax.fori_loop(1, 2 * NR, greet, 0)

    in_own = pltpu.make_async_copy(owner, own_v, i_sem.at[0])
    in_mass = pltpu.make_async_copy(mass, mass_v, i_sem.at[1])
    in_snap = pltpu.make_async_copy(snap, sall.at[c, z], i_sem.at[2])
    in_own.start()
    in_mass.start()
    in_snap.start()

    before = jnp.where(
        lax.broadcasted_iota(jnp.int32, (ND, ND), 0) < lax.broadcasted_iota(jnp.int32, (ND, ND), 1), 1.0, 0.0
    ).astype(BF16)
    in_own.wait()
    own = own_v[...].astype(F32)
    mine = onehot(own, NR)
    counts = jnp.dot(mine, before, preferred_element_type=F32)
    rank = jnp.sum(mine.astype(F32) * counts, axis=0, keepdims=True)
    row = lax.broadcasted_iota(jnp.int32, (16, 128), 0)
    code = jnp.zeros((16, 128), F32)
    for i in range(4):
        code = jnp.where(row == i, own[:, 128 * i : 128 * i + 128], code)
        code = jnp.where(row == i + 4, rank[:, 128 * i : 128 * i + 128], code)
    code = code.astype(BF16)
    odd = lax.rem(z, 2)
    in_mass.wait()
    for a in range(NR):
        msg[a, 0:16, :] = mass_v[jnp.where(odd == 1, a // 2, a)]
        msg[a, 16:32, :] = code
    raw[s] = msg[s]
    in_snap.wait()

    pl.semaphore_wait(barrier, 2 * NR - 1 + 7)

    def scatter(i, carry):
        a = lax.rem(s + i, NR)
        to(msg.at[a], raw.at[s], t_send, t_recv, blk, a).start()
        return carry

    lax.fori_loop(1, NR, scatter, 0)

    def ring(k, h, right):
        ref = sall.at[c, zmove(1 - k if right else k - 1), pl.ds(CH * h, CH)]
        rs = r_recv if right else l_recv
        return to(ref, ref, z_send, rs.at[k - 1, h], yl * NZ + zmove(1 if right else -1), s)

    def on_ring(k, h, right):
        return k < 8 or right == (h < NCH // 2)

    def sibling(k):
        for slot in {0: (0,), 8: (8,)}.get(k, (-k, k)):
            ref = sall.at[c, zmove(slot)]
            to(ref, ref, s_send, s_recv.at[max(k - 5, 0)], blk, sib).start()

    def ring_step(k):
        for h in range(NCH):
            for right in (True, False):
                if on_ring(k, h, right):
                    ref = sall.at[c, zmove(-k if right else k), pl.ds(CH * h, CH)]
                    drain(ref, (r_recv if right else l_recv).at[k - 1, h])
                    if k < 8 and on_ring(k + 1, h, right):
                        ring(k + 1, h, right).start()
        sibling(k)

    for h in range(NCH):
        for right in (True, False):
            ring(1, h, right).start()
    sibling(0)

    def halo_copy(dyl, ds):
        return to(
            sall.at[c, z], halo.at[2 - 2 * ds + yl], h_send, h_recv, lax.rem(yl + dyl, 2) * NZ + z, s + ds
        )

    for ds in (0, -1, 1):
        for dyl in (0, 1):
            if ds == 0:
                if dyl == 1:
                    halo_copy(dyl, ds).start()
            else:
                pl.when(jnp.logical_and(s + ds >= 0, s + ds < NR))(
                    lambda dyl=dyl, ds=ds: halo_copy(dyl, ds).start()
                )
    halo[2 + yl] = sall[c, z]

    useful = jnp.logical_or(odd == 0, lax.rem(s, 2) == 0)
    kind = jnp.where(odd == 1, 0, jnp.where(s < 8, 1, 2))
    part = jnp.where(odd == 1, s // 2, lax.rem(s, 8))
    shift = jnp.where(odd == 1, 1, jnp.where(s < 8, 0, -1))
    col = jnp.clip(yl * 8 + z // 2 + shift, 0, NR - 1)
    drain(raw.at[0:15], t_recv)

    @pl.when(useful)
    def _():
        own_c, rank_c = codes_of(raw, col)
        slices = raw[:, 0:16, :].reshape(256, 128)
        picked = jnp.dot(slices, onehot(rank_c, 128), preferred_element_type=F32)
        kept = jnp.zeros((16, ND), F32)
        for d in range(NR):
            kept = jnp.where(own_c == float(d), picked[16 * d : 16 * d + 16, :], kept)
        mz[z // 4] = kept.astype(BF16)
        for k in (8, 4, -4):
            to(mz.at[z // 4], mz.at[z // 4], a_send, a_recv, yl * NZ + zmove(k), s).start()

    ring_step(1)
    ring_step(2)

    def spread(f_remote, f_local):
        def each(m, carry):
            cc = yl * 8 + (lax.rem(z, 4) + 4 * m) // 2 + shift
            fits = jnp.logical_and(useful, jnp.logical_and(cc >= 0, cc < NR))
            dst = cbuf.at[kind, part]
            for dyl in range(2):
                here = jnp.logical_and(cc == s, dyl == 0)
                pl.when(jnp.logical_and(fits, jnp.logical_not(here)))(
                    lambda dyl=dyl: f_remote(
                        to(mz.at[m], dst, c_send.at[m, dyl], c_recv, lax.rem(yl + dyl, 2) * NZ + z, cc)
                    )
                )
                if f_local is not None and dyl == 0:
                    pl.when(jnp.logical_and(fits, here))(
                        lambda: f_local(pltpu.make_async_copy(mz.at[m], dst, c_recv))
                    )
            return carry

        lax.fori_loop(0, 4, each, 0)

    pl.when(useful)(lambda: drain(mz.at[0:3], a_recv))
    spread(lambda copy: copy.start(), lambda copy: copy.start())
    ring_step(3)
    ring_step(4)

    got = jnp.where(lax.rem(z, 2) == 0, jnp.where(lax.rem(z - 2 * s + 64, 4) == 0, 1, 2), 0)
    has = jnp.logical_and(
        jnp.logical_or(lax.rem(z, 2) == 0, lax.rem(z - 2 * s + 65, 4) == 0),
        jnp.logical_and(jnp.logical_or(got != 0, s > 0), jnp.logical_or(got != 2, s < NR - 1)),
    )
    got = jnp.where(has, got, 3)

    @pl.when(has)
    def _():
        drain(cbuf.at[0], c_recv)
        for k in (2, 1, -1):
            to(cbuf.at[got], cbuf.at[got], b_send, b_recv.at[got], yl * NZ + zmove(k), s).start()

    ring_step(5)

    acc[...] = jnp.zeros_like(acc)
    own_s, _ = codes_of(raw, s)
    hot_s = onehot(own_s, NR)
    edge = jnp.logical_or(s == 0, s == NR - 1)
    pl.when(edge)(lambda: drain(halo.at[0:3], h_recv))
    pl.when(jnp.logical_not(edge))(lambda: drain(halo.at[0:5], h_recv))

    def weigh(j):
        @pl.when(jnp.logical_and(s - 1 + j >= 0, s - 1 + j < NR))
        def _():
            pl.when(got != j)(lambda: drain(cbuf.at[j], b_recv.at[j]))
            own_j, rank_j = codes_of(raw, s - 1 + j)
            same = lax.dot_general(onehot(own_j, NR), hot_s, T0, preferred_element_type=F32)
            wide = lax.dot_general(onehot(rank_j, 128), cbuf[j].reshape(128, ND), T0, preferred_element_type=F32)
            m = (wide * same).astype(BF16)
            acc[...] += jnp.dot(halo[2 * j : 2 * j + 2].reshape(2 * SD, ND), m, preferred_element_type=F32)

    weigh(0)
    weigh(1)
    weigh(2)
    wown[...] = acc[...].reshape(2, SD, ND).astype(BF16)
    to(wown.at[1 - c], wc.at[c], w_send, w_recv, blk, sib).start()
    wc[c] = wown[c]
    ring_step(6)
    drain(wc.at[0], w_recv)

    def tile(slot):
        zz = zmove(slot)
        g = lax.dot_general(sall[0, zz], wc[0], T1, preferred_element_type=F32)
        gt[zz] = g + lax.dot_general(sall[1, zz], wc[1], T1, preferred_element_type=F32)
        late = lax.rem(zz // 2 - z // 2 + 10, 8) // 4
        home = x * 4 + lax.rem(zz // 4, 2) * 2 + lax.rem(zz // 2, 2)
        dst = yrecv.at[yl, yh, zz // 8, lax.rem(zz, 2)]
        far = jnp.logical_or(home != s, c != yl)
        pl.when(far)(lambda: to(gt.at[zz], dst, y_send, y_recv.at[late], c * NZ + z, home).start())
        pl.when(jnp.logical_not(far))(lambda: pltpu.make_async_copy(gt.at[zz], dst, y_recv.at[late]).start())

    drain(sall.at[0, 0:11], s_recv.at[0])
    for k in range(6):
        for slot in (0,) if k == 0 else (-k, k):
            tile(slot)
    drain(sall.at[0, 0:2], s_recv.at[1])
    tile(-6)
    tile(6)
    ring_step(7)
    drain(sall.at[0, 0:2], s_recv.at[2])
    tile(-7)
    tile(7)
    ring_step(8)
    drain(sall.at[0, 0:1], s_recv.at[3])
    tile(8)

    first = 2 * yh + c
    first = jnp.where(lax.rem(first - z // 2 + 10, 8) < 4, 0, 1)
    for late in range(2):
        i = lax.rem(first + late, 2)
        drain(yrecv.at[0:1], y_recv.at[late])
        for y in range(2):
            dest = 2 * y + i
            xsend[dest] = (yrecv[y, 0, i] + yrecv[y, 1, i]).reshape(256, 128)
            pl.when(x != dest)(
                lambda dest=dest: to(
                    xsend.at[dest], xrecv.at[x], x_send, x_recv, blk, 4 * dest + 2 * yh + c
                ).start()
            )
    xrecv[x] = xsend[x]
    drain(xrecv.at[0:3], x_recv)
    out[...] = (xrecv[0] + xrecv[1]) + (xrecv[2] + xrecv[3])

    drain(msg.at[0:15], t_send)
    pl.when(useful)(lambda: drain(mz.at[0:3], a_send))
    spread(lambda copy: copy.wait_send(), None)
    pl.when(has)(lambda: drain(cbuf, b_send))
    pl.when(edge)(lambda: drain(halo.at[0:3], h_send))
    pl.when(jnp.logical_not(edge))(lambda: drain(halo.at[0:5], h_send))
    drain(sall.at[0, 0:15], z_send)
    drain(sall.at[0], s_send)
    drain(wc.at[0], w_send)
    pl.when(c == yl)(lambda: drain(gt.at[0:12], y_send))
    pl.when(c != yl)(lambda: drain(gt, y_send))
    drain(xsend.at[0:3], x_send)


def per_device(snapshots, node_owner, mass_blocks, mass_cols):
    dma = pltpu.SemaphoreType.DMA
    one = dma(())
    return pl.pallas_call(
        kernel,
        out_shape=jax.ShapeDtypeStruct((256, 128), F32),
        in_specs=[pl.BlockSpec(memory_space=pl.ANY)] * 3,
        out_specs=pl.BlockSpec(memory_space=pltpu.VMEM),
        scratch_shapes=[
            pltpu.VMEM((1, ND), jnp.int32),
            pltpu.VMEM((16, 16, 128), BF16),
            pltpu.VMEM((16, 32, 128), BF16),
            pltpu.VMEM((16, 32, 128), BF16),
            pltpu.VMEM((4, 16, ND), BF16),
            pltpu.VMEM((3, 8, 16, ND), BF16),
            pltpu.VMEM((6, SD, ND), BF16),
            pltpu.VMEM((2, NZ, SD, ND), BF16),
            pltpu.VMEM((2 * SD, ND), F32),
            pltpu.VMEM((2, SD, ND), BF16),
            pltpu.VMEM((2, SD, ND), BF16),
            pltpu.VMEM((NZ, 128, 128), F32),
            pltpu.VMEM((2, 2, 2, 2, 128, 128), F32),
            pltpu.VMEM((4, 256, 128), F32),
            pltpu.VMEM((4, 256, 128), F32),
            dma((3,)), one, one, one, one, one, dma((3,)), dma((4, 2)), one,
            one, one, one, dma((8, NCH)), dma((8, NCH)), one, dma((4,)),
            one, one, one, dma((2,)), one, one,
        ],
        compiler_params=pltpu.CompilerParams(
            collective_id=0, has_side_effects=True, vmem_limit_bytes=64 * 1024 * 1024 - 64 * 1024
        ),
        cost_estimate=pl.CostEstimate(flops=1200000000, bytes_accessed=400000, transcendentals=0),
    )(snapshots, node_owner.reshape(1, ND), mass_blocks.reshape(16, 16, 128))


def solution(mesh):
    placed = (P("blk", "rows"), P("rows", None), P("rows", "blk", None, None), P("rows", "blk"))
    return jax.shard_map(
        per_device, mesh=mesh, in_specs=placed, out_specs=P("rows", "blk"), check_vma=False
    )
```

time: 83 us -> 72.4 us (0.87)
  the two profiles are of different devices: /device:TPU:69 before, /device:TPU:49 now
where the time goes in v2:
time: 72.4 us; the launch traced here: 72.2 us
  Pallas kernels  70.6 us (98%)
  local copies, waits for them, and re-layouts  1.57 us (2%)
    pallas_call x1, Pallas kernels, per_device(): pl.pallas_call(kernel, out_shape=jax.ShapeDtypeStruct((256, 128), F32), i...  70.6 us
    unnamed x1, local copies, waits for them, and re-layouts  1.57 us

profile of v2, /device:TPU:49, one launch (start us, length us, event | category | flops | bytes accessed | tf_op | source)
XLA Modules:
  0.0 72.2 jit_solution(271412302322595621)
XLA Ops:
  0.0 70.6 %shard_map.37 = f32[256,128]{1,0:T(8,128)} custom-call(bf16[128,512]{1,0:T(8,128)(2,1)} %snap.1, s32[1,512]{1,0:T(1,128)} %bitcast.3, bf16[16,16,128]{2,1,0:T(8,128)(2,1)} %bitcast.2), custom_call_target="tpu_custom_call" | custom-call | flops 1200000000 | bytes 400000 | tf_op jit(solution)/shard_map/pallas_call | solution.py:300
  70.7 1.6 %copy.5 = f32[256,128]{1,0:T(8,128)} copy(f32[256,128]{1,0:T(8,128)} %shard_map.37) | data formatting | bytes 262144

commit v3 on v2

--- a/solution.py
+++ b/solution.py
@@ -14,6 +14,7 @@
 SD = 128
 NCH = 4
 CH = SD // NCH
+FULL = 32767.0
 T0 = (((0,), (0,)), ((), ()))
 T1 = (((1,), (1,)), ((), ()))
 
@@ -30,9 +31,22 @@
     return jnp.where(ids == row, 1.0, 0.0).astype(BF16)
 
 
+def encode(g, ref, *at):
+    top = jnp.clip(jnp.max(jnp.abs(g), axis=0, keepdims=True), 1e-30, 1e30)
+    e = jnp.ceil(jnp.log2(top))
+    q = jnp.round(g * (FULL * jnp.exp2(-e)))
+    ref[(*at, slice(0, 256), slice(None))] = q.astype(jnp.int32).astype(jnp.int16)
+    ref[(*at, slice(256, 272), slice(None))] = jnp.broadcast_to(e, (16, 128)).astype(jnp.int32).astype(jnp.int16)
+
+
+def decode(v):
+    e = v[256:272, :].astype(jnp.int32).astype(F32)[0:1, :]
+    return v[0:256, :].astype(jnp.int32).astype(F32) * (jnp.exp2(e) * (1.0 / FULL))
+
+
 def kernel(
     snap, owner, mass, out,
-    own_v, mass_v, msg, raw, mz, cbuf, halo, sall, acc, wown, wc, gt, yrecv, xsend, xrecv,
+    own_v, mass_v, msg, raw, mz, cbuf, halo, sall, acc, wown, wc, gt, yrecv, xsend, xrecv, xown,
     i_sem, t_send, t_recv, a_send, a_recv, b_send, b_recv, c_send, c_recv,
     h_send, h_recv, z_send, r_recv, l_recv, s_send, s_recv,
     w_send, w_recv, y_send, y_recv, x_send, x_recv,
@@ -116,7 +130,7 @@
     def sibling(k):
         for slot in {0: (0,), 8: (8,)}.get(k, (-k, k)):
             ref = sall.at[c, zmove(slot)]
-            to(ref, ref, s_send, s_recv.at[max(k - 5, 0)], blk, sib).start()
+            to(ref, ref, s_send, s_recv.at[max(k // 2 - 2, 0)], blk, sib).start()
 
     def ring_step(k):
         for h in range(NCH):
@@ -237,48 +251,52 @@
     ring_step(6)
     drain(wc.at[0], w_recv)
 
-    def tile(slot):
-        zz = zmove(slot)
-        g = lax.dot_general(sall[0, zz], wc[0], T1, preferred_element_type=F32)
-        gt[zz] = g + lax.dot_general(sall[1, zz], wc[1], T1, preferred_element_type=F32)
-        late = lax.rem(zz // 2 - z // 2 + 10, 8) // 4
-        home = x * 4 + lax.rem(zz // 4, 2) * 2 + lax.rem(zz // 2, 2)
-        dst = yrecv.at[yl, yh, zz // 8, lax.rem(zz, 2)]
+    def tile(d):
+        u = lax.rem(z // 2 + d + 8, 8)
+        pair = pl.ds(2 * u, 2)
+        g = lax.dot_general(sall[0, pair].reshape(2 * SD, ND), wc[0], T1, preferred_element_type=F32)
+        g += lax.dot_general(sall[1, pair].reshape(2 * SD, ND), wc[1], T1, preferred_element_type=F32)
+        encode(g, gt, u)
+        late = 0 if -2 <= d < 2 else 1
+        home = x * 4 + lax.rem(u, 4)
+        dst = yrecv.at[yl, yh, u // 4]
         far = jnp.logical_or(home != s, c != yl)
-        pl.when(far)(lambda: to(gt.at[zz], dst, y_send, y_recv.at[late], c * NZ + z, home).start())
-        pl.when(jnp.logical_not(far))(lambda: pltpu.make_async_copy(gt.at[zz], dst, y_recv.at[late]).start())
+        pl.when(far)(lambda: to(gt.at[u], dst, y_send, y_recv.at[late], c * NZ + z, home).start())
+        pl.when(jnp.logical_not(far))(lambda: pltpu.make_async_copy(gt.at[u], dst, y_recv.at[late]).start())
 
     drain(sall.at[0, 0:11], s_recv.at[0])
-    for k in range(6):
-        for slot in (0,) if k == 0 else (-k, k):
-            tile(slot)
-    drain(sall.at[0, 0:2], s_recv.at[1])
-    tile(-6)
-    tile(6)
+    for d in (0, -1, 1, -2, 2):
+        tile(d)
     ring_step(7)
-    drain(sall.at[0, 0:2], s_recv.at[2])
-    tile(-7)
-    tile(7)
+    drain(sall.at[0, 0:4], s_recv.at[1])
+    tile(-3)
+    tile(3)
     ring_step(8)
-    drain(sall.at[0, 0:1], s_recv.at[3])
-    tile(8)
-
-    first = 2 * yh + c
-    first = jnp.where(lax.rem(first - z // 2 + 10, 8) < 4, 0, 1)
+    drain(sall.at[0, 0:1], s_recv.at[2])
+    tile(4)
+
+    first = jnp.where(lax.rem(2 * yh + c - z // 2 + 10, 8) < 4, 0, 1)
     for late in range(2):
         i = lax.rem(first + late, 2)
-        drain(yrecv.at[0:1], y_recv.at[late])
+        drain(yrecv.at[0, :, 0:2], y_recv.at[late])
         for y in range(2):
             dest = 2 * y + i
-            xsend[dest] = (yrecv[y, 0, i] + yrecv[y, 1, i]).reshape(256, 128)
-            pl.when(x != dest)(
-                lambda dest=dest: to(
-                    xsend.at[dest], xrecv.at[x], x_send, x_recv, blk, 4 * dest + 2 * yh + c
-                ).start()
-            )
-    xrecv[x] = xsend[x]
+            total = decode(yrecv[y, 0, i]) + decode(yrecv[y, 1, i])
+
+            @pl.when(x == dest)
+            def _():
+                xown[...] = total
+
+            @pl.when(x != dest)
+            def _():
+                encode(total, xsend, dest)
+                to(xsend.at[dest], xrecv.at[x], x_send, x_recv, blk, 4 * dest + 2 * yh + c).start()
+
     drain(xrecv.at[0:3], x_recv)
-    out[...] = (xrecv[0] + xrecv[1]) + (xrecv[2] + xrecv[3])
+    total = xown[...]
+    for k in range(1, 4):
+        total += decode(xrecv[lax.rem(x + k, 4)])
+    out[...] = total
 
     drain(msg.at[0:15], t_send)
     pl.when(useful)(lambda: drain(mz.at[0:3], a_send))
@@ -289,7 +307,7 @@
     drain(sall.at[0, 0:15], z_send)
     drain(sall.at[0], s_send)
     drain(wc.at[0], w_send)
-    pl.when(c == yl)(lambda: drain(gt.at[0:12], y_send))
+    pl.when(c == yl)(lambda: drain(gt.at[0:6], y_send))
     pl.when(c != yl)(lambda: drain(gt, y_send))
     drain(xsend.at[0:3], x_send)
 
@@ -314,12 +332,13 @@
             pltpu.VMEM((2 * SD, ND), F32),
             pltpu.VMEM((2, SD, ND), BF16),
             pltpu.VMEM((2, SD, ND), BF16),
-            pltpu.VMEM((NZ, 128, 128), F32),
-            pltpu.VMEM((2, 2, 2, 2, 128, 128), F32),
-            pltpu.VMEM((4, 256, 128), F32),
-            pltpu.VMEM((4, 256, 128), F32),
+            pltpu.VMEM((8, 272, 128), jnp.int16),
+            pltpu.VMEM((2, 2, 2, 272, 128), jnp.int16),
+            pltpu.VMEM((4, 272, 128), jnp.int16),
+            pltpu.VMEM((4, 272, 128), jnp.int16),
+            pltpu.VMEM((256, 128), F32),
             dma((3,)), one, one, one, one, one, dma((3,)), dma((4, 2)), one,
-            one, one, one, dma((8, NCH)), dma((8, NCH)), one, dma((4,)),
+            one, one, one, dma((8, NCH)), dma((8, NCH)), one, dma((3,)),
             one, one, one, dma((2,)), one, one,
         ],
         compiler_params=pltpu.CompilerParams(

time: 72.4 us -> 67.4 us (0.931)
  the two profiles are of different devices: /device:TPU:49 before, /device:TPU:6 now
where the time goes in v3:
time: 67.4 us; the launch traced here: 67.2 us
  Pallas kernels  65.7 us (97%)
  local copies, waits for them, and re-layouts  1.57 us (2%)
    pallas_call x1, Pallas kernels, per_device(): pl.pallas_call(kernel, out_shape=jax.ShapeDtypeStruct((256, 128), F32), i...  65.7 us
    unnamed x1, local copies, waits for them, and re-layouts  1.57 us

profile of v3, /device:TPU:6, one launch (start us, length us, event | category | flops | bytes accessed | tf_op | source)
XLA Modules:
  0.0 67.2 jit_solution(11122039311105261819)
XLA Ops:
  0.0 65.7 %shard_map.37 = f32[256,128]{1,0:T(8,128)} custom-call(bf16[128,512]{1,0:T(8,128)(2,1)} %snap.1, s32[1,512]{1,0:T(1,128)} %bitcast.3, bf16[16,16,128]{2,1,0:T(8,128)(2,1)} %bitcast.2), custom_call_target="tpu_custom_call" | custom-call | flops 1200000000 | bytes 400000 | tf_op jit(solution)/shard_map/pallas_call | solution.py:318
  65.7 1.6 %copy.5 = f32[256,128]{1,0:T(8,128)} copy(f32[256,128]{1,0:T(8,128)} %shard_map.37) | data formatting | bytes 262144

commit v4 on v3

--- a/solution.py
+++ b/solution.py
@@ -49,7 +49,7 @@
     own_v, mass_v, msg, raw, mz, cbuf, halo, sall, acc, wown, wc, gt, yrecv, xsend, xrecv, xown,
     i_sem, t_send, t_recv, a_send, a_recv, b_send, b_recv, c_send, c_recv,
     h_send, h_recv, z_send, r_recv, l_recv, s_send, s_recv,
-    w_send, w_recv, y_send, y_recv, x_send, x_recv,
+    w_send, w_recv, y_send, y_recv, x_send, x_recv, f_sem,
 ):
     blk, s = lax.axis_index("blk"), lax.axis_index("rows")
     yl, z = blk // NZ, lax.rem(blk, NZ)
@@ -68,7 +68,7 @@
         pltpu.make_async_copy(ref, ref, sem).wait()
 
     barrier = pltpu.get_barrier_semaphore()
-    for k in (8, 4, -4, 2, -2, 1, -1):
+    for k in (2, -2, 1, -1):
         pl.semaphore_signal(barrier, inc=1, device_id=(yl * NZ + zmove(k), s), device_id_type=MESH)
     plane = yl * NR + s
 
@@ -110,7 +110,16 @@
     raw[s] = msg[s]
     in_snap.wait()
 
-    pl.semaphore_wait(barrier, 2 * NR - 1 + 7)
+    pl.semaphore_wait(barrier, 2 * NR - 1 + 4)
+
+    def round_signal(n):
+        for k in (2, -2):
+            pl.semaphore_signal(f_sem.at[n], inc=1, device_id=(yl * NZ + zmove(k), s), device_id_type=MESH)
+
+    def round_wait(n):
+        pl.semaphore_wait(f_sem.at[n], 2)
+
+    round_signal(0)
 
     def scatter(i, carry):
         a = lax.rem(s + i, NR)
@@ -162,13 +171,20 @@
                     lambda dyl=dyl, ds=ds: halo_copy(dyl, ds).start()
                 )
     halo[2 + yl] = sall[c, z]
+    round_wait(0)
+    round_signal(1)
 
     useful = jnp.logical_or(odd == 0, lax.rem(s, 2) == 0)
     kind = jnp.where(odd == 1, 0, jnp.where(s < 8, 1, 2))
     part = jnp.where(odd == 1, s // 2, lax.rem(s, 8))
     shift = jnp.where(odd == 1, 1, jnp.where(s < 8, 0, -1))
     col = jnp.clip(yl * 8 + z // 2 + shift, 0, NR - 1)
+    round_wait(1)
+    round_signal(2)
+    ring_step(1)
     drain(raw.at[0:15], t_recv)
+
+    round_wait(2)
 
     @pl.when(useful)
     def _():
@@ -182,8 +198,8 @@
         for k in (8, 4, -4):
             to(mz.at[z // 4], mz.at[z // 4], a_send, a_recv, yl * NZ + zmove(k), s).start()
 
-    ring_step(1)
     ring_step(2)
+    ring_step(3)
 
     def spread(f_remote, f_local):
         def each(m, carry):
@@ -207,7 +223,6 @@
 
     pl.when(useful)(lambda: drain(mz.at[0:3], a_recv))
     spread(lambda copy: copy.start(), lambda copy: copy.start())
-    ring_step(3)
     ring_step(4)
 
     got = jnp.where(lax.rem(z, 2) == 0, jnp.where(lax.rem(z - 2 * s + 64, 4) == 0, 1, 2), 0)
@@ -240,11 +255,12 @@
             same = lax.dot_general(onehot(own_j, NR), hot_s, T0, preferred_element_type=F32)
             wide = lax.dot_general(onehot(rank_j, 128), cbuf[j].reshape(128, ND), T0, preferred_element_type=F32)
             m = (wide * same).astype(BF16)
-            acc[...] += jnp.dot(halo[2 * j : 2 * j + 2].reshape(2 * SD, ND), m, preferred_element_type=F32)
-
-    weigh(0)
-    weigh(1)
-    weigh(2)
+            acc[...] += jnp.dot(halo[pl.ds(2 * j, 2)].reshape(2 * SD, ND), m, preferred_element_type=F32)
+
+    kinds = [lax.rem(jnp.where(has, got, 0) + n, 3) for n in range(3)]
+    weigh(kinds[0])
+    weigh(kinds[1])
+    weigh(kinds[2])
     wown[...] = acc[...].reshape(2, SD, ND).astype(BF16)
     to(wown.at[1 - c], wc.at[c], w_send, w_recv, blk, sib).start()
     wc[c] = wown[c]
@@ -339,7 +355,7 @@
             pltpu.VMEM((256, 128), F32),
             dma((3,)), one, one, one, one, one, dma((3,)), dma((4, 2)), one,
             one, one, one, dma((8, NCH)), dma((8, NCH)), one, dma((3,)),
-            one, one, one, dma((2,)), one, one,
+            one, one, one, dma((2,)), one, one, pltpu.SemaphoreType.REGULAR((3,)),
         ],
         compiler_params=pltpu.CompilerParams(
             collective_id=0, has_side_effects=True, vmem_limit_bytes=64 * 1024 * 1024 - 64 * 1024

time: 67.4 us -> 65.6 us (0.973)
  Pallas kernels: 65.7 us -> 63.9 us
    pallas_call x1, Pallas kernels: 65.7 us -> 63.9 us  [per_device(): pl.pallas_call(kernel, out_shape=jax.ShapeDtypeStruct((256, 128), F32), i...]
where the time goes in v4:
time: 65.6 us; the launch traced here: 65.5 us
  Pallas kernels  63.9 us (97%)
  local copies, waits for them, and re-layouts  1.57 us (2%)
    pallas_call x1, Pallas kernels, per_device(): pl.pallas_call(kernel, out_shape=jax.ShapeDtypeStruct((256, 128), F32), i...  63.9 us
    unnamed x1, local copies, waits for them, and re-layouts  1.57 us

profile of v4, /device:TPU:6, one launch (start us, length us, event | category | flops | bytes accessed | tf_op | source)
XLA Modules:
  0.0 65.5 jit_solution(592637073538735015)
XLA Ops:
  0.0 63.9 %shard_map.37 = f32[256,128]{1,0:T(8,128)} custom-call(bf16[128,512]{1,0:T(8,128)(2,1)} %snap.1, s32[1,512]{1,0:T(1,128)} %bitcast.3, bf16[16,16,128]{2,1,0:T(8,128)(2,1)} %bitcast.2), custom_call_target="tpu_custom_call" | custom-call | flops 1200000000 | bytes 400000 | tf_op jit(solution)/shard_map/pallas_call | solution.py:334
  63.9 1.6 %copy.5 = f32[256,128]{1,0:T(8,128)} copy(f32[256,128]{1,0:T(8,128)} %shard_map.37) | data formatting | bytes 262144

commit v5 on v4

--- a/solution.py
+++ b/solution.py
@@ -47,7 +47,7 @@
 def kernel(
     snap, owner, mass, out,
     own_v, mass_v, msg, raw, mz, cbuf, halo, sall, acc, wown, wc, gt, yrecv, xsend, xrecv, xown,
-    i_sem, t_send, t_recv, a_send, a_recv, b_send, b_recv, c_send, c_recv,
+    i_sem, t_send, t_recv, a_send, a_recv, c_send, c_recv,
     h_send, h_recv, z_send, r_recv, l_recv, s_send, s_recv,
     w_send, w_recv, y_send, y_recv, x_send, x_recv, f_sem,
 ):
@@ -113,11 +113,11 @@
     pl.semaphore_wait(barrier, 2 * NR - 1 + 4)
 
     def round_signal(n):
-        for k in (2, -2):
+        for k in (2, -2, 1, -1) if n == 0 else (2, -2):
             pl.semaphore_signal(f_sem.at[n], inc=1, device_id=(yl * NZ + zmove(k), s), device_id_type=MESH)
 
     def round_wait(n):
-        pl.semaphore_wait(f_sem.at[n], 2)
+        pl.semaphore_wait(f_sem.at[n], 4 if n == 0 else 2)
 
     round_signal(0)
 
@@ -201,43 +201,34 @@
     ring_step(2)
     ring_step(3)
 
-    def spread(f_remote, f_local):
+    def spread(f):
         def each(m, carry):
             cc = yl * 8 + (lax.rem(z, 4) + 4 * m) // 2 + shift
-            fits = jnp.logical_and(useful, jnp.logical_and(cc >= 0, cc < NR))
-            dst = cbuf.at[kind, part]
-            for dyl in range(2):
-                here = jnp.logical_and(cc == s, dyl == 0)
-                pl.when(jnp.logical_and(fits, jnp.logical_not(here)))(
-                    lambda dyl=dyl: f_remote(
-                        to(mz.at[m], dst, c_send.at[m, dyl], c_recv, lax.rem(yl + dyl, 2) * NZ + z, cc)
-                    )
+            pl.when(jnp.logical_and(useful, jnp.logical_and(cc >= 0, cc < NR)))(lambda: f(m, cc))
+            return carry
+
+        lax.fori_loop(0, 4, each, 0)
+
+    def spread_start(m, cc):
+        dst = cbuf.at[kind, part]
+        for k in (2, 1, -1, 0):
+            for dyl in (1, 0):
+                copy = to(
+                    mz.at[m], dst, c_send.at[m], c_recv.at[kind], lax.rem(yl + dyl, 2) * NZ + zmove(k), cc
                 )
-                if f_local is not None and dyl == 0:
-                    pl.when(jnp.logical_and(fits, here))(
-                        lambda: f_local(pltpu.make_async_copy(mz.at[m], dst, c_recv))
-                    )
-            return carry
-
-        lax.fori_loop(0, 4, each, 0)
+                if k == 0 and dyl == 0:
+                    pl.when(cc != s)(lambda copy=copy: copy.start())
+                    pl.when(cc == s)(lambda: pltpu.make_async_copy(mz.at[m], dst, c_recv.at[kind]).start())
+                else:
+                    copy.start()
+
+    def spread_sent(m, cc):
+        pl.when(cc == s)(lambda: drain(cbuf.at[0, 0:7], c_send.at[m]))
+        pl.when(cc != s)(lambda: drain(cbuf.at[0], c_send.at[m]))
 
     pl.when(useful)(lambda: drain(mz.at[0:3], a_recv))
-    spread(lambda copy: copy.start(), lambda copy: copy.start())
+    spread(spread_start)
     ring_step(4)
-
-    got = jnp.where(lax.rem(z, 2) == 0, jnp.where(lax.rem(z - 2 * s + 64, 4) == 0, 1, 2), 0)
-    has = jnp.logical_and(
-        jnp.logical_or(lax.rem(z, 2) == 0, lax.rem(z - 2 * s + 65, 4) == 0),
-        jnp.logical_and(jnp.logical_or(got != 0, s > 0), jnp.logical_or(got != 2, s < NR - 1)),
-    )
-    got = jnp.where(has, got, 3)
-
-    @pl.when(has)
-    def _():
-        drain(cbuf.at[0], c_recv)
-        for k in (2, 1, -1):
-            to(cbuf.at[got], cbuf.at[got], b_send, b_recv.at[got], yl * NZ + zmove(k), s).start()
-
     ring_step(5)
 
     acc[...] = jnp.zeros_like(acc)
@@ -250,17 +241,16 @@
     def weigh(j):
         @pl.when(jnp.logical_and(s - 1 + j >= 0, s - 1 + j < NR))
         def _():
-            pl.when(got != j)(lambda: drain(cbuf.at[j], b_recv.at[j]))
+            drain(cbuf.at[j], c_recv.at[j])
             own_j, rank_j = codes_of(raw, s - 1 + j)
             same = lax.dot_general(onehot(own_j, NR), hot_s, T0, preferred_element_type=F32)
             wide = lax.dot_general(onehot(rank_j, 128), cbuf[j].reshape(128, ND), T0, preferred_element_type=F32)
             m = (wide * same).astype(BF16)
             acc[...] += jnp.dot(halo[pl.ds(2 * j, 2)].reshape(2 * SD, ND), m, preferred_element_type=F32)
 
-    kinds = [lax.rem(jnp.where(has, got, 0) + n, 3) for n in range(3)]
-    weigh(kinds[0])
-    weigh(kinds[1])
-    weigh(kinds[2])
+    weigh(0)
+    weigh(1)
+    weigh(2)
     wown[...] = acc[...].reshape(2, SD, ND).astype(BF16)
     to(wown.at[1 - c], wc.at[c], w_send, w_recv, blk, sib).start()
     wc[c] = wown[c]
@@ -316,8 +306,7 @@
 
     drain(msg.at[0:15], t_send)
     pl.when(useful)(lambda: drain(mz.at[0:3], a_send))
-    spread(lambda copy: copy.wait_send(), None)
-    pl.when(has)(lambda: drain(cbuf, b_send))
+    spread(spread_sent)
     pl.when(edge)(lambda: drain(halo.at[0:3], h_send))
     pl.when(jnp.logical_not(edge))(lambda: drain(halo.at[0:5], h_send))
     drain(sall.at[0, 0:15], z_send)
@@ -353,7 +342,7 @@
             pltpu.VMEM((4, 272, 128), jnp.int16),
             pltpu.VMEM((4, 272, 128), jnp.int16),
             pltpu.VMEM((256, 128), F32),
-            dma((3,)), one, one, one, one, one, dma((3,)), dma((4, 2)), one,
+            dma((3,)), one, one, one, one, dma((4,)), dma((3,)),
             one, one, one, dma((8, NCH)), dma((8, NCH)), one, dma((3,)),
             one, one, one, dma((2,)), one, one, pltpu.SemaphoreType.REGULAR((3,)),
         ],

time: 65.6 us -> 64.1 us (0.977)
  Pallas kernels: 63.9 us -> 62.4 us
    pallas_call x1, Pallas kernels: 63.9 us -> 62.4 us  [per_device(): pl.pallas_call(kernel, out_shape=jax.ShapeDtypeStruct((256, 128), F32), i...]
where the time goes in v5:
time: 64.1 us; the launch traced here: 64 us
  Pallas kernels  62.4 us (97%)
  local copies, waits for them, and re-layouts  1.57 us (2%)
    pallas_call x1, Pallas kernels, per_device(): pl.pallas_call(kernel, out_shape=jax.ShapeDtypeStruct((256, 128), F32), i...  62.4 us
    unnamed x1, local copies, waits for them, and re-layouts  1.57 us

profile of v5, /device:TPU:6, one launch (start us, length us, event | category | flops | bytes accessed | tf_op | source)
XLA Modules:
  0.0 64.0 jit_solution(205269513451179566)
XLA Ops:
  0.0 62.4 %shard_map.37 = f32[256,128]{1,0:T(8,128)} custom-call(bf16[128,512]{1,0:T(8,128)(2,1)} %snap.1, s32[1,512]{1,0:T(1,128)} %bitcast.3, bf16[16,16,128]{2,1,0:T(8,128)(2,1)} %bitcast.2), custom_call_target="tpu_custom_call" | custom-call | flops 1200000000 | bytes 400000 | tf_op jit(solution)/shard_map/pallas_call | solution.py:323
  62.4 1.6 %copy.5 = f32[256,128]{1,0:T(8,128)} copy(f32[256,128]{1,0:T(8,128)} %shard_map.37) | data formatting | bytes 262144

commit v6 on v5

--- a/solution.py
+++ b/solution.py
@@ -46,10 +46,10 @@
 
 def kernel(
     snap, owner, mass, out,
-    own_v, mass_v, msg, raw, mz, cbuf, halo, sall, acc, wown, wc, gt, yrecv, xsend, xrecv, xown,
+    own_v, mass_v, msg, raw, mz, cbuf, halo, sall, acc, wown, wc, gt, yrecv, xsend, xrecv, xown, drecv,
     i_sem, t_send, t_recv, a_send, a_recv, c_send, c_recv,
     h_send, h_recv, z_send, r_recv, l_recv, s_send, s_recv,
-    w_send, w_recv, y_send, y_recv, x_send, x_recv, f_sem,
+    w_send, w_recv, y_send, y_recv, x_send, x_recv, f_sem, d_send, d_recv,
 ):
     blk, s = lax.axis_index("blk"), lax.axis_index("rows")
     yl, z = blk // NZ, lax.rem(blk, NZ)
@@ -263,12 +263,14 @@
         g = lax.dot_general(sall[0, pair].reshape(2 * SD, ND), wc[0], T1, preferred_element_type=F32)
         g += lax.dot_general(sall[1, pair].reshape(2 * SD, ND), wc[1], T1, preferred_element_type=F32)
         encode(g, gt, u)
-        late = 0 if -2 <= d < 2 else 1
-        home = x * 4 + lax.rem(u, 4)
-        dst = yrecv.at[yl, yh, u // 4]
+        if d == 4:
+            home, dst, ssem, rsem = (2 * yl + u // 4) * 4 + lax.rem(u, 4), drecv.at[x, yh], d_send, d_recv
+        else:
+            home, dst, ssem = x * 4 + lax.rem(u, 4), yrecv.at[yl, yh, u // 4], y_send
+            rsem = y_recv.at[0 if -2 <= d < 2 else 1]
         far = jnp.logical_or(home != s, c != yl)
-        pl.when(far)(lambda: to(gt.at[u], dst, y_send, y_recv.at[late], c * NZ + z, home).start())
-        pl.when(jnp.logical_not(far))(lambda: pltpu.make_async_copy(gt.at[u], dst, y_recv.at[late]).start())
+        pl.when(far)(lambda: to(gt.at[u], dst, ssem, rsem, c * NZ + z, home).start())
+        pl.when(jnp.logical_not(far))(lambda: pltpu.make_async_copy(gt.at[u], dst, rsem).start())
 
     drain(sall.at[0, 0:11], s_recv.at[0])
     for d in (0, -1, 1, -2, 2):
@@ -277,12 +279,11 @@
     drain(sall.at[0, 0:4], s_recv.at[1])
     tile(-3)
     tile(3)
-    ring_step(8)
-    drain(sall.at[0, 0:1], s_recv.at[2])
-    tile(4)
-
     first = jnp.where(lax.rem(2 * yh + c - z // 2 + 10, 8) < 4, 0, 1)
-    for late in range(2):
+    last = lax.rem(z // 2, 4) == 2 * yh + c
+    direct = jnp.logical_and(last, lax.rem(x + first, 2) == 1)
+
+    def half(late):
         i = lax.rem(first + late, 2)
         drain(yrecv.at[0, :, 0:2], y_recv.at[late])
         for y in range(2):
@@ -298,11 +299,28 @@
                 encode(total, xsend, dest)
                 to(xsend.at[dest], xrecv.at[x], x_send, x_recv, blk, 4 * dest + 2 * yh + c).start()
 
-    drain(xrecv.at[0:3], x_recv)
-    total = xown[...]
-    for k in range(1, 4):
-        total += decode(xrecv[lax.rem(x + k, 4)])
-    out[...] = total
+    ring_step(8)
+    half(0)
+    drain(sall.at[0, 0:1], s_recv.at[2])
+    tile(4)
+
+    pl.when(jnp.logical_not(last))(lambda: half(1))
+
+    @pl.when(direct)
+    def _():
+        drain(drecv, d_recv)
+        total = decode(drecv[0, 0]) + decode(drecv[0, 1])
+        for k in range(1, 4):
+            total += decode(drecv[k, 0]) + decode(drecv[k, 1])
+        out[...] = total
+
+    @pl.when(jnp.logical_not(direct))
+    def _():
+        drain(xrecv.at[0:3], x_recv)
+        total = xown[...]
+        for k in range(1, 4):
+            total += decode(xrecv[lax.rem(x + k, 4)])
+        out[...] = total
 
     drain(msg.at[0:15], t_send)
     pl.when(useful)(lambda: drain(mz.at[0:3], a_send))
@@ -312,9 +330,16 @@
     drain(sall.at[0, 0:15], z_send)
     drain(sall.at[0], s_send)
     drain(wc.at[0], w_send)
-    pl.when(c == yl)(lambda: drain(gt.at[0:6], y_send))
-    pl.when(c != yl)(lambda: drain(gt, y_send))
-    drain(xsend.at[0:3], x_send)
+    own_y = c == yl
+    pl.when(jnp.logical_not(own_y))(lambda: drain(gt.at[0:7], y_send))
+    pl.when(jnp.logical_and(own_y, last))(lambda: drain(gt.at[0:6], y_send))
+    pl.when(jnp.logical_and(own_y, jnp.logical_not(last)))(lambda: drain(gt.at[0:5], y_send))
+    u_last = lax.rem(z // 2 + 4, 8)
+    self_last = jnp.logical_and(own_y, (2 * yl + u_last // 4) * 4 + lax.rem(u_last, 4) == s)
+    pl.when(jnp.logical_not(self_last))(lambda: drain(gt.at[0], d_send))
+    pl.when(jnp.logical_not(last))(lambda: drain(xsend.at[0:3], x_send))
+    pl.when(direct)(lambda: drain(xsend.at[0:2], x_send))
+    pl.when(jnp.logical_and(last, jnp.logical_not(direct)))(lambda: drain(xsend.at[0], x_send))
 
 
 def per_device(snapshots, node_owner, mass_blocks, mass_cols):
@@ -342,12 +367,14 @@
             pltpu.VMEM((4, 272, 128), jnp.int16),
             pltpu.VMEM((4, 272, 128), jnp.int16),
             pltpu.VMEM((256, 128), F32),
+            pltpu.VMEM((4, 2, 272, 128), jnp.int16),
             dma((3,)), one, one, one, one, dma((4,)), dma((3,)),
             one, one, one, dma((8, NCH)), dma((8, NCH)), one, dma((3,)),
             one, one, one, dma((2,)), one, one, pltpu.SemaphoreType.REGULAR((3,)),
+            one, one,
         ],
         compiler_params=pltpu.CompilerParams(
-            collective_id=0, has_side_effects=True, vmem_limit_bytes=64 * 1024 * 1024 - 64 * 1024
+            collective_id=0, has_side_effects=True, vmem_limit_bytes=54976 * 1024
         ),
         cost_estimate=pl.CostEstimate(flops=1200000000, bytes_accessed=400000, transcendentals=0),
     )(snapshots, node_owner.reshape(1, ND), mass_blocks.reshape(16, 16, 128))

time: 64.1 us -> 64.3 us (level)
  the two profiles are of different devices: /device:TPU:6 before, /device:TPU:2 now
where the time goes in v6:
time: 64.3 us; the launch traced here: 64.1 us
  Pallas kernels  61.9 us (96%)
  local copies, waits for them, and re-layouts  2.18 us (3%)
    pallas_call x1, Pallas kernels, per_device(): pl.pallas_call(kernel, out_shape=jax.ShapeDtypeStruct((256, 128), F32), i...  61.9 us
    unnamed x5, local copies, waits for them, and re-layouts  2.18 us

profile of v6, /device:TPU:2, one launch (start us, length us, event | category | flops | bytes accessed | tf_op | source)
XLA Modules:
  0.0 64.1 jit_solution(965933338980363304)
XLA Ops:
  0.0 0.0 copy-start.1
  0.0 0.7 %copy-done.1 = s32[512,1]{0,1:T(1,128)S(1)} copy-done((s32[512,1]{0,1:T(1,128)S(1)}, s32[512,1]{0,1:T(1,128)}, u32[]{:S(2)}) %copy-start.1) | copy-done | bytes 2072
  0.7 0.0 copy-start
  0.7 0.8 %copy-done = bf16[1,2,128,128]{3,2,1,0:T(8,128)(2,1)S(1)} copy-done((bf16[1,2,128,128]{3,2,1,0:T(8,128)(2,1)S(1)}, bf16[1,2,128,128]{3,2,1,0:T(8,128)(2,1)}, u32[]{:S(2)}) %copy-start) | copy-done | bytes 65560
  1.5 61.9 %shard_map.37 = f32[256,128]{1,0:T(8,128)S(1)} custom-call(bf16[128,512]{1,0:T(8,128)(2,1)} %snap.1, s32[1,512]{1,0:T(1,128)S(1)} %bitcast.3, bf16[16,16,128]{2,1,0:T(8,128)(2,1)S(1)} %bitcast.2), custom_call_target="tpu_custom_call" | custom-call | flops 1200000000 | bytes 400000 | tf_op jit(solution)/shard_map/pallas_call | solution.py:348
  63.4 0.7 %copy.5 = f32[256,128]{1,0:T(8,128)} copy(f32[256,128]{1,0:T(8,128)S(1)} %shard_map.37) | data formatting | bytes 262144
Async XLA Ops:
  0.0 0.7 %copy-start.1 = (s32[512,1]{0,1:T(1,128)S(1)}, s32[512,1]{0,1:T(1,128)}, u32[]{:S(2)}) copy-start(s32[512,1]{0,1:T(1,128)} %param.5) | copy-start | bytes 6148
  0.7 0.8 %copy-start = (bf16[1,2,128,128]{3,2,1,0:T(8,128)(2,1)S(1)}, bf16[1,2,128,128]{3,2,1,0:T(8,128)(2,1)}, u32[]{:S(2)}) copy-start(bf16[1,2,128,128]{3,2,1,0:T(8,128)(2,1)} %param.6) | copy-start | bytes 196612

commit v7 on v6

--- a/solution.py
+++ b/solution.py
@@ -161,15 +161,6 @@
             sall.at[c, z], halo.at[2 - 2 * ds + yl], h_send, h_recv, lax.rem(yl + dyl, 2) * NZ + z, s + ds
         )
 
-    for ds in (0, -1, 1):
-        for dyl in (0, 1):
-            if ds == 0:
-                if dyl == 1:
-                    halo_copy(dyl, ds).start()
-            else:
-                pl.when(jnp.logical_and(s + ds >= 0, s + ds < NR))(
-                    lambda dyl=dyl, ds=ds: halo_copy(dyl, ds).start()
-                )
     halo[2 + yl] = sall[c, z]
     round_wait(0)
     round_signal(1)
@@ -198,6 +189,15 @@
         for k in (8, 4, -4):
             to(mz.at[z // 4], mz.at[z // 4], a_send, a_recv, yl * NZ + zmove(k), s).start()
 
+    for ds in (0, -1, 1):
+        for dyl in (0, 1):
+            if ds == 0:
+                if dyl == 1:
+                    halo_copy(dyl, ds).start()
+            else:
+                pl.when(jnp.logical_and(s + ds >= 0, s + ds < NR))(
+                    lambda dyl=dyl, ds=ds: halo_copy(dyl, ds).start()
+                )
     ring_step(2)
     ring_step(3)
 

time: 64.3 us -> 64.2 us (level)
  the two profiles are of different devices: /device:TPU:2 before, /device:TPU:6 now
where the time goes in v7:
time: 64.2 us; the launch traced here: 63.4 us
  Pallas kernels  61.2 us (95%)
  local copies, waits for them, and re-layouts  2.18 us (3%)
    pallas_call x1, Pallas kernels, per_device(): pl.pallas_call(kernel, out_shape=jax.ShapeDtypeStruct((256, 128), F32), i...  61.2 us
    unnamed x5, local copies, waits for them, and re-layouts  2.18 us

profile of v7, /device:TPU:6, one launch (start us, length us, event | category | flops | bytes accessed | tf_op | source)
XLA Modules:
  0.0 63.4 jit_solution(10000921605783922136)
XLA Ops:
  0.0 0.0 copy-start.1
  0.0 0.7 %copy-done.1 = s32[512,1]{0,1:T(1,128)S(1)} copy-done((s32[512,1]{0,1:T(1,128)S(1)}, s32[512,1]{0,1:T(1,128)}, u32[]{:S(2)}) %copy-start.1) | copy-done | bytes 2072
  0.7 0.0 copy-start
  0.7 0.8 %copy-done = bf16[1,2,128,128]{3,2,1,0:T(8,128)(2,1)S(1)} copy-done((bf16[1,2,128,128]{3,2,1,0:T(8,128)(2,1)S(1)}, bf16[1,2,128,128]{3,2,1,0:T(8,128)(2,1)}, u32[]{:S(2)}) %copy-start) | copy-done | bytes 65560
  1.5 61.2 %shard_map.37 = f32[256,128]{1,0:T(8,128)S(1)} custom-call(bf16[128,512]{1,0:T(8,128)(2,1)} %snap.1, s32[1,512]{1,0:T(1,128)S(1)} %bitcast.3, bf16[16,16,128]{2,1,0:T(8,128)(2,1)S(1)} %bitcast.2), custom_call_target="tpu_custom_call" | custom-call | flops 1200000000 | bytes 400000 | tf_op jit(solution)/shard_map/pallas_call | solution.py:348
  62.8 0.7 %copy.5 = f32[256,128]{1,0:T(8,128)} copy(f32[256,128]{1,0:T(8,128)S(1)} %shard_map.37) | data formatting | bytes 262144
Async XLA Ops:
  0.0 0.7 %copy-start.1 = (s32[512,1]{0,1:T(1,128)S(1)}, s32[512,1]{0,1:T(1,128)}, u32[]{:S(2)}) copy-start(s32[512,1]{0,1:T(1,128)} %param.5) | copy-start | bytes 6148
  0.7 0.8 %copy-start = (bf16[1,2,128,128]{3,2,1,0:T(8,128)(2,1)S(1)}, bf16[1,2,128,128]{3,2,1,0:T(8,128)(2,1)}, u32[]{:S(2)}) copy-start(bf16[1,2,128,128]{3,2,1,0:T(8,128)(2,1)} %param.6) | copy-start | bytes 196612
